TPU v7x, 512 devices: a whole 4x4x16 slice. The times are simulated.
512 devices in a mesh: gx: 32 (over z, core), gy: 16 (over y, x).
Axes of the slice: x: 4, y: 4, z: 16, core: 2. Of those that a mesh axis runs over, the one named last changes fastest.
Arguments:
- loads: bfloat16 [32, 16, 384, 128], P('gx', 'gy'), may hold values from -6 to 6
- schur: bfloat16 [32, 16, 768, 768], P('gx', 'gy'), as said below
- local_inv: bfloat16 [32, 16, 768, 768], P('gx', 'gy'), as said below
- coarse_basis: bfloat16 [32, 16, 12, 768], P('gx', 'gy'), may hold values from -0.21875 to 0.21875
- coarse_index: int32 [32, 16, 12], P('gx', 'gy'), may hold values from 0 to 3071, as said below
- face_nodes: int32 [32, 16, 2], P('gx', 'gy'), may hold values from 16 to 64, as said below
- coarse_inverse: float32 [3072, 3072], P('gy', 'gx'), as said below
Outputs:
- solution: float32 [32, 16, 384, 128], P('gx', 'gy')
- preconditioned: float32 [32, 16, 384, 128], P('gx', 'gy')
Inputs may be any that keep to these rules, and one draw needn't show every extreme that they name: `face_nodes`: live nodes of each owned face; the faces on the slab's outer edge are clamped whatever the count says. Some face has all 64 nodes. For c < 3, coarse_index[a, b, 3 + c] and coarse_index[a, b, 9 + c] number the averages of the east and north faces of (a, b); coarse_index[a, b, c] = coarse_index[a - 1, b, 3 + c] and coarse_index[a, b, 6 + c] = coarse_index[a, b - 1, 9 + c], with a - 1 taken modulo 32 and b - 1 modulo 16. Every coarse unknown is named by exactly two primal unknowns. `schur`: symmetric positive definite. `local_inv`: symmetric positive definite. `coarse_inverse`: symmetric positive definite.
All inputs are finite; a program needn't handle non-finite values.
Results may differ from a plain program's by a relative error of at most 0.024.
Values may be sent and summed in bfloat16 or wider, within the bound.
A program may use at most 64 MiB of HBM per device.

v0:
```python
import jax
import jax.numpy as jnp
from jax import lax
from jax.sharding import PartitionSpec as P

ITERS = 2


def shifted(block, axis, distance):
    devices = range(lax.axis_size(axis))
    route = [(i - distance, i) for i in devices if i - distance in devices]
    return lax.ppermute(block, axis, route)


def shards(loads, schur, local_inv, coarse_basis, coarse_index, face_nodes, coarse_inverse):
    highest = lax.Precision.HIGHEST
    face_rows = schur.shape[-1] // 4
    node_count = face_rows // 3
    row_pos = lax.axis_index("gx")
    col_pos = lax.axis_index("gy")
    node_of = jnp.arange(face_rows) % node_count
    live_nodes = node_of[None, :] < face_nodes[0, 0][:, None]
    inside = jnp.stack([row_pos < lax.axis_size("gx") - 1, col_pos < lax.axis_size("gy") - 1])
    live_mask = (live_nodes & inside[:, None]).astype(jnp.float32).reshape(2 * face_rows, 1)
    schur_mat = schur[0, 0]
    inverse_mat = local_inv[0, 0]
    basis_rows = coarse_basis[0, 0]
    index_list = coarse_index[0, 0]
    block_rows = coarse_inverse.shape[0]
    block_cols = coarse_inverse.shape[1]
    total_rows = block_rows * lax.axis_size("gy")
    col_start = row_pos * block_cols

    def restrict(vector):
        east_face = vector[:face_rows]
        north_face = vector[face_rows:]
        west_face = shifted(east_face, "gx", 1)
        south_face = shifted(north_face, "gy", 1)
        return jnp.concatenate([west_face, east_face, south_face, north_face], axis=0)

    def extend(local_vals):
        from_right = shifted(local_vals[:face_rows].astype(jnp.bfloat16), "gx", -1).astype(
            jnp.float32
        )
        from_above = shifted(
            local_vals[2 * face_rows : 3 * face_rows].astype(jnp.bfloat16), "gy", -1
        ).astype(jnp.float32)
        east_face = local_vals[face_rows : 2 * face_rows] + from_right
        north_face = local_vals[3 * face_rows :] + from_above
        return jnp.concatenate([east_face, north_face], axis=0) * live_mask

    def inner_product(first_arr, second_arr):
        return lax.psum(jnp.sum(first_arr * second_arr, axis=0), ("gx", "gy"))

    def listed(primal):
        return (
            lax.all_gather(primal, ("gx", "gy"), axis=0, tiled=True),
            lax.all_gather(index_list, ("gx", "gy"), axis=0, tiled=True),
        )

    def coarse_pick(primal):
        all_values, all_owners = listed(primal)
        load_cases = all_values.shape[1]
        coarse_rhs = jnp.zeros((total_rows, load_cases), jnp.float32).at[all_owners].add(all_values)
        rhs_slice = lax.dynamic_slice_in_dim(coarse_rhs, col_start, block_cols, 0)
        partial_sol = jnp.dot(coarse_inverse, rhs_slice, precision=highest)
        block_sol = lax.psum(partial_sol, "gx")
        coarse_sol = lax.all_gather(
            block_sol.astype(jnp.bfloat16), "gy", axis=0, tiled=True
        ).astype(block_sol.dtype)
        return jnp.take(coarse_sol, index_list, axis=0)

    def precondition(residual):
        local_rows = restrict(residual.astype(jnp.bfloat16))
        local_part = jnp.dot(inverse_mat, local_rows, preferred_element_type=jnp.float32)
        primal = jnp.dot(basis_rows, local_rows, preferred_element_type=jnp.float32)
        picked = coarse_pick(primal).astype(jnp.bfloat16)
        spread = jnp.dot(basis_rows.T, picked, preferred_element_type=jnp.float32)
        return extend(local_part + spread)

    residual = loads[0, 0].astype(jnp.float32) * live_mask
    solution = jnp.zeros_like(residual)
    precond = precondition(residual)
    direction = precond
    current = inner_product(residual, precond)
    for iteration in range(ITERS):
        operate_local_rows = restrict(direction.astype(jnp.bfloat16))
        mapped = extend(jnp.dot(schur_mat, operate_local_rows, preferred_element_type=jnp.float32))
        step_size = current / inner_product(direction, mapped)
        solution = solution + step_size * direction
        residual = residual - step_size * mapped
        precond = precondition(residual)
        if iteration + 1 < ITERS:
            updated = inner_product(residual, precond)
            direction = precond + updated / current * direction
            current = updated
    return (solution[None, None], precond[None, None])


def solution(mesh):
    placed = (
        P("gx", "gy", None, None),
        P("gx", "gy", None, None),
        P("gx", "gy", None, None),
        P("gx", "gy", None, None),
        P("gx", "gy", None),
        P("gx", "gy", None),
        P("gy", "gx"),
    )
    return jax.shard_map(
        shards,
        mesh=mesh,
        in_specs=placed,
        out_specs=(P("gx", "gy", None, None), P("gx", "gy", None, None)),
        check_vma=False,
    )
```

profile of v0, /device:TPU:1, one launch (start us, length us, event | category | flops | bytes accessed | tf_op | source)
XLA Modules:
  0.0 1480.4 jit_solution(15067047494456279077)
XLA Ops:
  9.4 4.9 collective-permute-start
  21.2 111.0 %all-reduce = s32[6144]{0:T(1024)S(1)} all-reduce(s32[6144]{0:T(1024)S(1)} %get-tuple-element.46), channel_id=2, replica_groups=mesh['gx'=32,'gy'=16] {'gx','gy'}, use_global_device_ids=true, to_apply=%add | all-reduce | flops 6144 | bytes 49152 | tf_op jit(solution)/shard_map/all_gather | solution.py:58
  132.9 90.3 %all-gather.8.cloned.1.call-done = f32[512,12,128]{2,1,0:T(8,128)} async-done(((f32[1,12,128]{2,1,0:T(8,128)}), f32[512,12,128]{2,1,0:T(8,128)}) %all-gather.8.cloned.1.call-update) | async-done | bytes 3145744 | tf_op jit(solution)/shard_map/all_gather | solution.py:57
  223.1 4.6 reshape.332
  227.7 33.9 %scatter_custom_fusion = f32[3072,128]{1,0:T(8,128)S(1)} fusion(s32[6144]{0:T(1024)S(1)} %compare_select_fusion, f32[6144,128]{1,0:T(8,128)} %reshape.332, f32[]{:T(128)} %constant.46.clone.1), kind=kCustom, calls=%fused_computation.29 | custom fusion | flops 786432 | bytes 1573376 | tf_op jit(solution)/shard_map/scatter-add | solution.py:64
  261.8 88.6 %psum.49 = bf16[192,128]{1,0:T(8,128)(2,1)S(1)} all-reduce(f32[192,128]{1,0:T(8,128)S(1)} %convolution_bitcast_fusion.4), channel_id=1, replica_groups=mesh['gx'=32,'gy'=16] {'gx'}, use_global_device_ids=true, to_apply=%region_1.2 | all-reduce | flops 24576 | bytes 147456 | tf_op jit(solution)/shard_map/psum | solution.py:67
  350.4 19.3 %all_gather.25 = bf16[3072,128]{1,0:T(8,128)(2,1)S(1)} all-gather(bf16[192,128]{1,0:T(8,128)(2,1)S(1)} %psum.49), channel_id=1, replica_groups=mesh['gx'=32,'gy'=16] {'gy'}, dimensions={0}, use_global_device_ids=true | all-gather | bytes 835584 | tf_op jit(solution)/shard_map/all_gather | solution.py:68
  371.2 10.3 collective-permute-start.2
  382.9 4.4 collective-permute-done.3
  394.2 3.3 collective-permute-start.6
  399.8 3.6 collective-permute-done.7
  403.7 104.5 %all-reduce.1 = (f32[128]{0:T(128)S(1)}, f32[128]{0:T(128)S(1)}) all-reduce(f32[128]{0:T(128)S(1)} %get-tuple-element.10, f32[128]{0:T(128)S(1)} %get-tuple-element.9), channel_id=1, replica_groups=mesh['gx'=32,'gy'=16] {'gx','gy'}, use_global_device_ids=true, to_apply=%region_3.5 | all-reduce | flops 256 | bytes 2048 | tf_op jit(solution)/shard_map/psum | solution.py:53
  508.5 4.2 collective-permute-start.8
  517.9 193.6 %all-gather.10.cloned.1.call-done = f32[512,12,128]{2,1,0:T(8,128)} async-done(((f32[1,12,128]{2,1,0:T(8,128)}), f32[512,12,128]{2,1,0:T(8,128)}) %all-gather.10.cloned.1.call-update) | async-done | bytes 3145744 | tf_op jit(solution)/shard_map/all_gather | solution.py:57
  711.6 4.6 reshape.334
  716.1 34.7 %scatter_custom_fusion.1 = f32[3072,128]{1,0:T(8,128)} fusion(s32[6144]{0:T(1024)S(1)} %compare_select_fusion, f32[6144,128]{1,0:T(8,128)} %reshape.334, f32[]{:T(128)} %constant.46.clone.1), kind=kCustom, calls=%fused_computation.27 | custom fusion | flops 786432 | bytes 1573376 | tf_op jit(solution)/shard_map/scatter-add | solution.py:64
  751.9 88.6 %psum.52 = bf16[192,128]{1,0:T(8,128)(2,1)S(1)} all-reduce(f32[192,128]{1,0:T(8,128)S(1)} %convolution_bitcast_fusion.3), channel_id=1, replica_groups=mesh['gx'=32,'gy'=16] {'gx'}, use_global_device_ids=true, to_apply=%region_7.9 | all-reduce | flops 24576 | bytes 147456 | tf_op jit(solution)/shard_map/psum | solution.py:67
  840.5 20.9 %all_gather.27 = bf16[3072,128]{1,0:T(8,128)(2,1)} all-gather(bf16[192,128]{1,0:T(8,128)(2,1)S(1)} %psum.52), channel_id=1, replica_groups=mesh['gx'=32,'gy'=16] {'gy'}, dimensions={0}, use_global_device_ids=true | all-gather | bytes 835584 | tf_op jit(solution)/shard_map/all_gather | solution.py:68
  864.9 10.6 collective-permute-start.10
  876.8 4.4 collective-permute-done.11
  881.6 101.4 %psum.53 = f32[128]{0:T(128)S(1)} all-reduce(f32[128]{0:T(128)S(1)} %multiply_reduce_fusion.1), channel_id=1, replica_groups=mesh['gx'=32,'gy'=16] {'gx','gy'}, use_global_device_ids=true, to_apply=%region_9.11 | all-reduce | flops 128 | bytes 1024 | tf_op jit(solution)/shard_map/psum | solution.py:53
  983.2 4.2 collective-permute-start.12
  987.5 3.1 collective-permute-start.13
  1000.2 103.2 %psum.54 = f32[128]{0:T(128)S(1)} all-reduce(f32[128]{0:T(128)S(1)} %multiply_reduce_fusion), channel_id=1, replica_groups=mesh['gx'=32,'gy'=16] {'gx','gy'}, use_global_device_ids=true, to_apply=%region_11.13 | all-reduce | flops 128 | bytes 1024 | tf_op jit(solution)/shard_map/psum | solution.py:53
  1103.7 3.4 collective-permute-start.16
  1111.9 194.3 %all-gather.12.cloned.1.call-done = f32[512,12,128]{2,1,0:T(8,128)} async-done(((f32[1,12,128]{2,1,0:T(8,128)}), f32[512,12,128]{2,1,0:T(8,128)}) %all-gather.12.cloned.1.call-update) | async-done | bytes 3145744 | tf_op jit(solution)/shard_map/all_gather | solution.py:57
  1306.2 4.6 reshape.336
  1310.7 34.7 %scatter_custom_fusion.2 = f32[3072,128]{1,0:T(8,128)} fusion(s32[6144]{0:T(1024)S(1)} %compare_select_fusion, f32[6144,128]{1,0:T(8,128)} %reshape.336, f32[]{:T(128)} %constant.46.clone.1), kind=kCustom, calls=%fused_computation.25 | custom fusion | flops 786432 | bytes 1573376 | tf_op jit(solution)/shard_map/scatter-add | solution.py:64
  1346.5 88.6 %psum.55 = bf16[192,128]{1,0:T(8,128)(2,1)S(1)} all-reduce(f32[192,128]{1,0:T(8,128)S(1)} %convolution_bitcast_fusion.2), channel_id=1, replica_groups=mesh['gx'=32,'gy'=16] {'gx'}, use_global_device_ids=true, to_apply=%region_13.15 | all-reduce | flops 24576 | bytes 147456 | tf_op jit(solution)/shard_map/psum | solution.py:67
  1435.1 19.3 %all_gather.29 = bf16[3072,128]{1,0:T(8,128)(2,1)S(1)} all-gather(bf16[192,128]{1,0:T(8,128)(2,1)S(1)} %psum.55), channel_id=1, replica_groups=mesh['gx'=32,'gy'=16] {'gy'}, dimensions={0}, use_global_device_ids=true | all-gather | bytes 835584 | tf_op jit(solution)/shard_map/all_gather | solution.py:68
  1455.8 10.3 collective-permute-start.18
  1467.5 4.4 collective-permute-done.19
  (99 shorter events, 54.3 us)
Async XLA Ops:
  7.2 363.4 %copy-start = (bf16[1,1,768,768]{3,2,1,0:T(8,128)(2,1)S(1)}, bf16[1,1,768,768]{3,2,1,0:T(8,128)(2,1)}, u32[]{:S(2)}) copy-start(bf16[1,1,768,768]{3,2,1,0:T(8,128)(2,1)} %param.11) | copy-start | bytes 3538948
  7.2 216.0 %all-gather.8.cloned.1.call-start = ((), (), s32[]{:S(2)}) async-start(), calls=%async_computation | async-start | bytes 4202496 | tf_op jit(solution)/shard_map/all_gather | solution.py:57
  9.4 8.9 collective-permute-start
  14.3 4.4 collective-permute-start.1
  20.4 691.2 %all-gather.10.cloned.1.call-start = ((), (), s32[]{:S(2)}) async-start(), calls=%async_computation.1 | async-start | bytes 4202496 | tf_op jit(solution)/shard_map/all_gather | solution.py:57
  227.7 33.9 %copy-start.2 = (f32[192,96]{1,0:T(8,128)S(1)}, f32[192,96]{1,0:T(8,128)}, u32[]{:S(2)}) copy-start(f32[192,96]{1,0:T(8,128)} %param.15) | copy-start | bytes 221188
  227.7 142.6 %copy-start.3 = (bf16[1,1,12,768]{3,2,1,0:T(8,128)(2,1)S(1)}, bf16[1,1,12,768]{3,2,1,0:T(8,128)(2,1)}, u32[]{:S(2)}) copy-start(bf16[1,1,12,768]{3,2,1,0:T(8,128)(2,1)} %param.12) | copy-start | bytes 55300
  370.6 23.0 %copy-start.1 = (bf16[1,1,768,768]{3,2,1,0:T(8,128)(2,1)S(1)}, bf16[1,1,768,768]{3,2,1,0:T(8,128)(2,1)}, u32[]{:S(2)}) copy-start(bf16[1,1,768,768]{3,2,1,0:T(8,128)(2,1)} %param.10) | copy-start | bytes 3538948
  371.2 11.6 collective-permute-start.2
  381.5 5.7 collective-permute-start.3
  387.6 4.8 collective-permute-start.4
  389.5 4.1 collective-permute-start.5
  394.2 5.6 collective-permute-start.6
  397.5 5.9 collective-permute-start.7
  508.5 7.2 collective-permute-start.8
  512.8 4.2 collective-permute-start.9
  517.0 199.1 %copy-start.4 = (bf16[192,128]{0,1:T(8,128)(2,1)}, bf16[192,128]{0,1:T(8,128)(2,1)S(1)}, u32[]{:S(2)}) copy-start(bf16[192,128]{0,1:T(8,128)(2,1)S(1)} %collective-permute-done.9) | copy-start | bytes 147460
  517.9 788.3 %all-gather.12.cloned.1.call-start = ((), (), s32[]{:S(2)}) async-start(), calls=%async_computation.2 | async-start | bytes 4202496 | tf_op jit(solution)/shard_map/all_gather | solution.py:57
  864.9 12.0 collective-permute-start.10
  875.5 5.7 collective-permute-start.11
  983.2 7.4 collective-permute-start.12
  987.5 4.5 collective-permute-start.13
  992.5 5.9 collective-permute-start.14
  994.4 5.3 collective-permute-start.15
  1103.7 6.0 collective-permute-start.16
  1107.1 3.9 collective-permute-start.17
  1455.8 11.6 collective-permute-start.18
  1466.2 5.7 collective-permute-start.19
Sparse Core Ops, SparseCore 0:
  20.5 202.6 all-gather.7
  518.0 193.5 all-gather.9
  1112.0 194.1 all-gather.11
where the time goes:
time: 1480 us
  blocking collectives  745 us (50%)
  waiting for transfers between devices  507 us (34%)
  other arithmetic  108 us (7%)
  starting transfers between devices  76.4 us (5%)
  local copies, waits for them, and re-layouts  19.9 us (1%)
    all_gather x3, waiting for transfers between devices, listed(): lax.all_gather(primal, ('gx', 'gy'), axis=0, tiled=True)  478 us
    psum x3, blocking collectives, inner_product(): return lax.psum(jnp.sum(first_arr * second_arr, axis=0), ('gx', 'gy'))  309 us
    psum x3, blocking collectives, coarse_pick(): block_sol = lax.psum(partial_sol, 'gx')  266 us
    all_gather x1, blocking collectives, listed(): lax.all_gather(index_list, ('gx', 'gy'), axis=0, tiled=True)  111 us
    scatter-add x3, other arithmetic, coarse_pick(): jnp.zeros((total_rows, load_cases), jnp.float32).at[all_owners]  103 us
    ppermute x20, starting transfers between devices, shifted(): return lax.ppermute(block, axis, route)  76.3 us
    all_gather x3, blocking collectives, coarse_pick(): lax.all_gather(block_sol.astype(jnp.bfloat16), 'gy', axis=0, tiled=True)  59.4 us
  transfers between devices with their start and end apart: 23, of which 16 were waited for; matrix products, arithmetic and copies ran while one was open for 0% of the time, Pallas kernels for 0%

commit v1 on v0

v1 whole, which is shorter than its diff:
```python
import functools
import jax
import jax.numpy as jnp
from jax import lax
from jax.experimental import pallas as pl
from jax.experimental.pallas import tpu as pltpu
from jax.sharding import PartitionSpec as P

MESH = pl.DeviceIdType.MESH
F32 = jnp.float32
BF16 = jnp.bfloat16
TILE = 16
CODE = 4096
MASK_LANE = 64
BT_LANES = 128
SOLVES = 3
OPS = 2


def kernel(
    n_gx,
    n_gy,
    loads,
    schur_hbm,
    linv_hbm,
    basis,
    index,
    nodes,
    cinv,
    sol_out,
    pre_out,
    schur,
    linv,
    bpad,
    bt_send,
    bt_recv,
    bb,
    masks,
    rows,
    name_msg,
    name_plane,
    name_gx,
    sel_t,
    strip,
    tsel,
    c2,
    t_val,
    t_send,
    t_recv,
    s_send,
    s_recv,
    g_msg,
    g_buf,
    xs,
    xr,
    x_msg,
    xb,
    ys,
    yr,
    pk,
    v0,
    v1,
    z1,
    w0,
    load_sem,
    face_send,
    face_recv,
    name_send,
    name_recv,
    strip_send,
    strip_recv,
    c2_send,
    c2_recv,
    stage_send,
    stage_recv,
    t_ssem,
    t_rsem,
    s_ssem,
    s_rsem,
    p_ssem,
    p_rsem,
):
    a = lax.axis_index("gx")
    b = lax.axis_index("gy")
    n_z = n_gx // 2
    n_plane = 2 * n_gy
    z = a // 2
    c = lax.rem(a, 2)
    slot = c * n_gy + b
    local = schur.shape[0]
    face = local // 4
    nodes_per = face // 3
    cr, cc = cinv.shape
    strip_w = 8 * n_gy
    nc = cr * n_gy
    load_cases = loads.shape[1]

    def plane_peer(k):
        other = lax.rem(slot + k, n_plane)
        return {"gx": 2 * z + other // n_gy, "gy": lax.rem(other, n_gy)}

    def signal(device):
        pl.semaphore_signal(barrier, inc=1, device_id=device, device_id_type=MESH)

    barrier = pltpu.get_barrier_semaphore()

    @pl.loop(1, n_plane)
    def _(k):
        signal(plane_peer(k))

    @pl.loop(1, n_gx)
    def _(k):
        other = lax.rem(a + k, n_gx)

        @pl.when(other // 2 != z)
        def _():
            signal({"gx": other, "gy": b})

    load_linv = pltpu.make_async_copy(linv_hbm, linv, load_sem.at[0])
    load_schur = pltpu.make_async_copy(schur_hbm, schur, load_sem.at[1])
    load_linv.start()
    load_schur.start()

    def remote(src, dst, send, recv, device):
        return pltpu.make_async_remote_copy(
            src_ref=src,
            dst_ref=dst,
            send_sem=send,
            recv_sem=recv,
            device_id=device,
            device_id_type=MESH,
        )

    def plane_send(src, dst, send, recv):
        @pl.loop(1, n_plane)
        def _(k):
            remote(src, dst.at[slot], send, recv, plane_peer(k)).start()

    def z_send(src, dst, send, recv):
        @pl.loop(1, n_z)
        def _(k):
            other = lax.rem(z + k, n_z)
            remote(
                src.at[other], dst.at[z], send, recv, {"gx": 2 * other + c, "gy": b}
            ).start()

    def wait_bytes(buf, count, sem):
        part = buf.at[pl.ds(0, count)]
        pltpu.make_async_copy(part, part, sem).wait()

    west = {"gx": lax.rem(a + n_gx - 1, n_gx), "gy": b}
    east = {"gx": lax.rem(a + 1, n_gx), "gy": b}
    south = {"gx": a, "gy": lax.rem(b + n_gy - 1, n_gy)}
    north = {"gx": a, "gy": lax.rem(b + 1, n_gy)}
    neighbours = ((west, 1), (east, 0), (south, 3), (north, 2))

    def face_rows(which):
        return pl.ds(which * face, face)

    def exchange(src, dst, send, recv):
        copies = []
        for mine, (device, theirs) in enumerate(neighbours):
            copies.append(
                remote(
                    src.at[face_rows(mine)],
                    dst.at[face_rows(theirs)],
                    send.at[mine],
                    recv.at[theirs],
                    device,
                )
            )
        for copy in copies:
            copy.start()
        return copies

    def finish(copies):
        for copy in copies:
            copy.wait_recv()

    lane = lax.broadcasted_iota(jnp.int32, (1, local), 1)
    which = lane // face
    node = lax.rem(lax.rem(lane, face), nodes_per)
    alive_east = (which == 1) & (node < nodes[0]) & (a < n_gx - 1)
    alive_north = (which == 3) & (node < nodes[1]) & (b < n_gy - 1)
    mask_row = jnp.where(alive_east | alive_north, 1.0, 0.0).astype(F32)
    basis_wide = basis[...].astype(F32)
    n_primal = basis_wide.shape[0]

    bpad[...] = jnp.zeros_like(bpad)
    bpad[TILE : TILE + n_primal, :] = basis_wide
    bpad[MASK_LANE : MASK_LANE + 1, :] = mask_row
    flipped = bpad[...].T
    bt_send[...] = flipped.astype(BF16)
    masks[...] = jnp.broadcast_to(flipped[:, MASK_LANE : MASK_LANE + 1], masks.shape)
    bpad[...] = jnp.zeros_like(bpad)
    bpad[0:n_primal, :] = basis_wide
    bb[...] = bpad[...].T.astype(BF16)
    basis16 = bpad[0:TILE, :].astype(BF16)

    rows[face : 2 * face, :] = (
        loads[0:face, :].astype(F32) * masks[face : 2 * face, :]
    ).astype(BF16)
    rows[3 * face :, :] = (
        loads[face:, :].astype(F32) * masks[3 * face :, :]
    ).astype(BF16)

    name_row = lax.broadcasted_iota(jnp.int32, name_msg.shape, 0)
    name_lane = lax.broadcasted_iota(jnp.int32, name_msg.shape, 1)
    names = CODE + name_row - n_primal
    for j in range(n_primal):
        names = jnp.where(name_row == j, index[j], names)
    half = name_msg.shape[1] // 2
    name_msg[...] = (
        jnp.where(name_lane < half, names // 64, lax.rem(names, 64)).astype(F32).astype(BF16)
    )
    name_plane[slot] = name_msg[...]
    name_gx[c * n_z + z] = name_msg[...]

    my_strip = strip.at[pl.ds(pl.multiple_of(b * cr, 8), cr)]
    wide = jnp.concatenate(
        [cinv[...].astype(BF16), jnp.zeros((cr, strip_w - cc), BF16)], axis=1
    )
    strip[pl.ds(pl.multiple_of(b * cr, 8), cr), :] = wide

    pl.semaphore_wait(barrier, n_plane - 1 + n_gx - 2)

    start_copies = []
    for mine, (device, theirs) in ((1, (east, 0)), (3, (north, 2))):
        copy = remote(
            rows.at[face_rows(mine)],
            rows.at[face_rows(theirs)],
            face_send.at[mine],
            face_recv.at[theirs],
            device,
        )
        copy.start()
        start_copies.append(copy)

    plane_send(name_msg, name_plane, name_send.at[0], name_recv.at[0])

    @pl.loop(1, n_gx)
    def _(k):
        other = lax.rem(a + k, n_gx)
        remote(
            name_msg,
            name_gx.at[c * n_z + z],
            name_send.at[1],
            name_recv.at[1],
            {"gx": other, "gy": b},
        ).start()

    @pl.loop(1, n_gy)
    def _(k):
        other = lax.rem(b + k, n_gy)
        remote(my_strip, my_strip, strip_send, strip_recv, {"gx": a, "gy": other}).start()

    bt_copies = exchange(bt_send, bt_recv, face_send.at[pl.ds(4, 4)], face_recv.at[pl.ds(4, 4)])

    def coarse_start(k, local_rows, sums):
        primal = jnp.dot(basis16, local_rows, preferred_element_type=F32)
        for j, value in enumerate(sums):
            at = lax.broadcasted_iota(jnp.int32, primal.shape, 0) == n_primal + j
            primal = jnp.where(at, value, primal)
        message = primal.astype(BF16)
        g_msg[k] = message
        g_buf[k, slot] = message
        plane_send(g_msg.at[k], g_buf.at[k], stage_send.at[k, 0], stage_recv.at[k, 0])
        t_val[...] = jnp.dot(linv[...], local_rows, preferred_element_type=F32)
        t_send[k] = t_val[...].astype(BF16)
        return exchange(t_send.at[k], t_recv.at[k], t_ssem.at[k], t_rsem.at[k])

    def coarse_scatter(k):
        wait_bytes(g_buf.at[k], n_plane - 1, stage_recv.at[k, 0])
        gathered = g_buf[k].reshape(n_plane * TILE, load_cases)
        part = jnp.dot(sel_t[...], gathered, preferred_element_type=F32)
        part = part.reshape(n_z, 8, load_cases)
        xs[k] = part
        xr[k, z] = xs[k, z]
        z_send(xs.at[k], xr.at[k], stage_send.at[k, 1], stage_recv.at[k, 1])

    def coarse_gather(k):
        wait_bytes(xr.at[k], n_z - 1, stage_recv.at[k, 1])
        mine = jnp.sum(xr[k], axis=0)
        x_msg[k] = mine
        xb[k, slot] = mine
        plane_send(x_msg.at[k], xb.at[k], stage_send.at[k, 2], stage_recv.at[k, 2])

    def coarse_solve(k):
        wait_bytes(xb.at[k], n_plane - 1, stage_recv.at[k, 2])
        low = xb[k, 0:n_gy].reshape(strip_w, load_cases).astype(BF16)
        high = xb[k, n_gy:].reshape(strip_w, load_cases).astype(BF16)
        part = jnp.dot(c2[0], low, preferred_element_type=F32) + jnp.dot(
            c2[1], high, preferred_element_type=F32
        )
        ys[k] = part.astype(BF16).reshape(n_z, TILE, load_cases)
        yr[k, z] = ys[k, z]
        z_send(ys.at[k], yr.at[k], stage_send.at[k, 3], stage_recv.at[k, 3])

    def sums_of(k):
        both = xb[k, cc // 8]
        return [both[j : j + 1, :] for j in range(4)]

    def coarse_finish(k):
        wait_bytes(yr.at[k], n_z - 1, stage_recv.at[k, 3])
        picked = jnp.sum(yr[k].astype(F32), axis=0).astype(BF16)
        for at in range(4):
            pk[k, at, 0:TILE] = picked
        copies = []
        for mine, (device, theirs) in enumerate(neighbours):
            copies.append(
                remote(
                    pk.at[k, mine, pl.ds(0, TILE)],
                    pk.at[k, theirs, pl.ds(TILE, TILE)],
                    p_ssem.at[k, mine],
                    p_rsem.at[k, theirs],
                    device,
                )
            )
        for copy in copies:
            copy.start()
        return copies

    def preconditioned(k, faces):
        parts = []
        for at in faces:
            here = face_rows(at)
            spread = jnp.dot(bb[here, 0 : 2 * TILE], pk[k, at], preferred_element_type=F32)
            total = t_val[here, :] + t_recv[k, here, :].astype(F32) + spread
            parts.append(total * masks[here, :])
        return parts

    def operate(k, vector):
        mapped = jnp.dot(schur[...], vector.astype(BF16), preferred_element_type=F32)
        s_send[k] = mapped.astype(BF16)
        copies = exchange(s_send.at[k], s_recv.at[k], s_ssem.at[k], s_rsem.at[k])
        finish(copies)
        return (mapped + s_recv[k].astype(F32)) * masks[...], copies

    def owned(first, second):
        total = first * second
        east_part = jnp.sum(total[face : 2 * face], axis=0, keepdims=True)
        north_part = jnp.sum(total[3 * face :], axis=0, keepdims=True)
        return east_part + north_part

    def split(value):
        high = value.astype(BF16).astype(F32)
        return high, value - high

    finish(start_copies)
    load_linv.wait()
    t_copies = [coarse_start(0, rows[...], [])]

    wait_bytes(name_plane, n_plane - 1, name_recv.at[0])
    plane_names = name_plane[...].reshape(n_plane * TILE, name_msg.shape[1]).astype(F32)
    plane_names = plane_names[:, 0:1] * 64.0 + plane_names[:, half : half + 1]
    target = lax.broadcasted_iota(jnp.int32, (1, 8 * n_z), 1)
    place = 8 * b + lax.rem(target, 8)
    wanted = jnp.where(place < cc, cc * (2 * (target // 8) + c) + place, CODE + place - cc)
    hits = jnp.where(plane_names == wanted.astype(F32), 1.0, 0.0).astype(F32)
    sel_t[...] = hits.T.astype(BF16)

    coarse_scatter(0)

    wait_bytes(name_gx, n_gx - 1, name_recv.at[1])
    gx_names = name_gx[...].reshape(n_gx * TILE, name_msg.shape[1]).astype(F32)
    gx_names = gx_names[:, 0:1] * 64.0 + gx_names[:, half : half + 1]
    wait_bytes(strip.reshape(n_gy, cr, strip_w), n_gy - 1, strip_recv)
    chunk = 256 if nc % 256 == 0 else nc // 3
    column = lax.broadcasted_iota(jnp.int32, (1, chunk), 1).astype(F32)

    def select(step, total):
        base = pl.multiple_of(step * chunk, chunk)
        hit = jnp.where(gx_names - (base * 1.0) == column, 1.0, 0.0).astype(BF16)
        return total + jnp.dot(hit, strip[pl.ds(base, chunk), :], preferred_element_type=F32)

    chosen = lax.fori_loop(
        0, nc // chunk, select, jnp.zeros((n_gx * TILE, strip_w), F32)
    )
    tsel[...] = chosen.astype(BF16).reshape(2, n_z * TILE, strip_w)
    c2[c] = tsel[c]
    c2_copy = remote(
        tsel.at[1 - c], c2.at[c], c2_send, c2_recv, {"gx": 2 * z + 1 - c, "gy": b}
    )
    c2_copy.start()

    coarse_gather(0)
    finish(bt_copies)
    bb[...] = bb[...] + bt_recv[...]
    masks[0:face, :] = jnp.broadcast_to(
        bt_recv[0:face, MASK_LANE : MASK_LANE + 1].astype(F32), (face, load_cases)
    )
    masks[2 * face : 3 * face, :] = jnp.broadcast_to(
        bt_recv[2 * face : 3 * face, MASK_LANE : MASK_LANE + 1].astype(F32),
        (face, load_cases),
    )
    c2_copy.wait_recv()
    coarse_solve(0)
    finish(t_copies[0])
    pk_copies = [coarse_finish(0)]
    finish(pk_copies[0])
    for at, part in enumerate(preconditioned(0, range(4))):
        v0[face_rows(at), :] = part

    load_schur.wait()
    first = v0[...]
    image, copies = operate(0, first)
    s_copies = [copies]
    w0[...] = image
    start = rows[...].astype(F32)
    old, curve = owned(start, first), owned(first, image)

    t_copies.append(coarse_start(1, image.astype(BF16), [*split(old), *split(curve)]))
    coarse_scatter(1)
    coarse_gather(1)
    coarse_solve(1)
    finish(t_copies[1])
    sums = sums_of(1)
    old = sums[0] + sums[1]
    curve = sums[2] + sums[3]
    step = old / curve
    pk_copies.append(coarse_finish(1))
    finish(pk_copies[1])
    for at, part in enumerate(preconditioned(1, range(4))):
        here = face_rows(at)
        v1[here, :] = part
        z1[here, :] = v0[here, :] - step * part

    second = z1[...]
    image, copies = operate(1, second)
    s_copies.append(copies)
    residual = rows[...].astype(F32) - step * w0[...]
    new = owned(residual, second)
    cross = owned(second, w0[...])
    high, low = split(owned(second, image))

    t_copies.append(coarse_start(2, image.astype(BF16), [new, high, low, cross]))
    coarse_scatter(2)
    coarse_gather(2)
    coarse_solve(2)
    finish(t_copies[2])
    sums = sums_of(2)
    new = sums[0]
    ratio = new / old
    step_two = new / (sums[1] + sums[2] + ratio * (2.0 * sums[3] + ratio * curve))
    pk_copies.append(coarse_finish(2))
    finish(pk_copies[2])
    for half_at, (at, part) in enumerate(zip((1, 3), preconditioned(2, (1, 3)))):
        here = face_rows(at)
        there = pl.ds(half_at * face, face)
        second = z1[here, :]
        direction = second + ratio * v0[here, :]
        sol_out[there, :] = step * v0[here, :] + step_two * direction
        pre_out[there, :] = second - step_two * (part + ratio * v1[here, :])

    for copy in start_copies + bt_copies + [c2_copy]:
        copy.wait_send()
    wait_bytes(name_plane, n_plane - 1, name_send.at[0])
    wait_bytes(name_gx, n_gx - 1, name_send.at[1])
    wait_bytes(strip.reshape(n_gy, cr, strip_w), n_gy - 1, strip_send)
    for k in range(SOLVES):
        for copy in t_copies[k] + pk_copies[k]:
            copy.wait_send()
        wait_bytes(g_buf.at[k], n_plane - 1, stage_send.at[k, 0])
        wait_bytes(xr.at[k], n_z - 1, stage_send.at[k, 1])
        wait_bytes(xb.at[k], n_plane - 1, stage_send.at[k, 2])
        wait_bytes(yr.at[k], n_z - 1, stage_send.at[k, 3])
    for k in range(OPS):
        for copy in s_copies[k]:
            copy.wait_send()


def shards(
    n_gx, n_gy, loads, schur, local_inv, coarse_basis, coarse_index, face_nodes, coarse_inverse
):
    owned, cases = loads.shape[2:]
    local = schur.shape[-1]
    cr, cc = coarse_inverse.shape
    nc = cr * n_gy
    n_z = n_gx // 2
    n_plane = 2 * n_gy
    strip_w = 8 * n_gy
    dma = pltpu.SemaphoreType.DMA
    vmem = pl.BlockSpec(memory_space=pltpu.VMEM)
    smem = pl.BlockSpec(memory_space=pltpu.SMEM)
    anywhere = pl.BlockSpec(memory_space=pl.ANY)
    scratch = [
        pltpu.VMEM((local, local), BF16),
        pltpu.VMEM((local, local), BF16),
        pltpu.VMEM((BT_LANES, local), F32),
        pltpu.VMEM((local, BT_LANES), BF16),
        pltpu.VMEM((local, BT_LANES), BF16),
        pltpu.VMEM((local, BT_LANES), BF16),
        pltpu.VMEM((local, cases), F32),
        pltpu.VMEM((local, cases), BF16),
        pltpu.VMEM((TILE, 128), BF16),
        pltpu.VMEM((n_plane, TILE, 128), BF16),
        pltpu.VMEM((n_gx, TILE, 128), BF16),
        pltpu.VMEM((8 * n_z, n_plane * TILE), BF16),
        pltpu.VMEM((nc, strip_w), BF16),
        pltpu.VMEM((2, n_z * TILE, strip_w), BF16),
        pltpu.VMEM((2, n_z * TILE, strip_w), BF16),
        pltpu.VMEM((local, cases), F32),
        pltpu.VMEM((SOLVES, local, cases), BF16),
        pltpu.VMEM((SOLVES, local, cases), BF16),
        pltpu.VMEM((OPS, local, cases), BF16),
        pltpu.VMEM((OPS, local, cases), BF16),
        pltpu.VMEM((SOLVES, TILE, cases), BF16),
        pltpu.VMEM((SOLVES, n_plane, TILE, cases), BF16),
        pltpu.VMEM((SOLVES, n_z, 8, cases), F32),
        pltpu.VMEM((SOLVES, n_z, 8, cases), F32),
        pltpu.VMEM((SOLVES, 8, cases), F32),
        pltpu.VMEM((SOLVES, n_plane, 8, cases), F32),
        pltpu.VMEM((SOLVES, n_z, TILE, cases), BF16),
        pltpu.VMEM((SOLVES, n_z, TILE, cases), BF16),
        pltpu.VMEM((SOLVES, 4, 2 * TILE, cases), BF16),
        pltpu.VMEM((local, cases), F32),
        pltpu.VMEM((local, cases), F32),
        pltpu.VMEM((local, cases), F32),
        pltpu.VMEM((local, cases), F32),
        dma((2,)),
        dma((8,)),
        dma((8,)),
        dma((2,)),
        dma((2,)),
        dma,
        dma,
        dma,
        dma,
        dma((SOLVES, 4)),
        dma((SOLVES, 4)),
        dma((SOLVES, 4)),
        dma((SOLVES, 4)),
        dma((OPS, 4)),
        dma((OPS, 4)),
        dma((SOLVES, 4)),
        dma((SOLVES, 4)),
    ]
    solution, precond = pl.pallas_call(
        functools.partial(kernel, n_gx, n_gy),
        out_shape=(
            jax.ShapeDtypeStruct((owned, cases), F32),
            jax.ShapeDtypeStruct((owned, cases), F32),
        ),
        in_specs=[vmem, anywhere, anywhere, vmem, smem, smem, vmem],
        out_specs=(vmem, vmem),
        scratch_shapes=scratch,
        compiler_params=pltpu.CompilerParams(
            collective_id=0, has_side_effects=True, vmem_limit_bytes=40 * 1024 * 1024
        ),
        name="bddc_cg",
    )(
        loads[0, 0],
        schur[0, 0],
        local_inv[0, 0],
        coarse_basis[0, 0],
        coarse_index[0, 0],
        face_nodes[0, 0],
        coarse_inverse,
    )
    return solution[None, None], precond[None, None]


def solution(mesh):
    placed = (
        P("gx", "gy", None, None),
        P("gx", "gy", None, None),
        P("gx", "gy", None, None),
        P("gx", "gy", None, None),
        P("gx", "gy", None),
        P("gx", "gy", None),
        P("gy", "gx"),
    )
    return jax.shard_map(
        functools.partial(shards, mesh.shape["gx"], mesh.shape["gy"]),
        mesh=mesh,
        in_specs=placed,
        out_specs=(P("gx", "gy", None, None), P("gx", "gy", None, None)),
        check_vma=False,
    )
```

time: 1480 us -> 150 us (0.10)
  blocking collectives: 745 us -> 0 us
  waiting for transfers between devices: 507 us -> 0 us
  Pallas kernels: 0 us -> 142 us
  other arithmetic: 108 us -> 0 us
  starting transfers between devices: 76.4 us -> 0 us
    psum x6 -> x0, blocking collectives: 575 us -> none  [the longest x3 309 us: inner_product(): return lax.psum(jnp.sum(first_arr * second_arr, axis=0), ('gx', 'gy'))]
    all_gather x3 -> x0, waiting for transfers between devices: 478 us -> none  [listed(): lax.all_gather(primal, ('gx', 'gy'), axis=0, tiled=True)]
    all_gather x4 -> x0, blocking collectives: 170 us -> none  [the longest x1 111 us: listed(): lax.all_gather(index_list, ('gx', 'gy'), axis=0, tiled=True)]
    pallas_call x0 -> x1, Pallas kernels: none -> 142 us  [shards(): pl.pallas_call(functools.partial(kernel, n_gx, n_gy), out_shape=(jax.Shap...]
    scatter-add x3 -> x0, other arithmetic: 103 us -> none  [coarse_pick(): jnp.zeros((total_rows, load_cases), jnp.float32).at[all_owners]]
    ppermute x20 -> x0, starting transfers between devices: 76.3 us -> none  [shifted(): return lax.ppermute(block, axis, route)]
    ppermute x20 -> x0, waiting for transfers between devices: 28.3 us -> none  [shifted(): return lax.ppermute(block, axis, route)]
  transfers between devices with their start and end apart: 23 -> 0, of which waited for: 16 -> 0; matrix products, arithmetic and copies ran while one was open for 0% -> 0% of each run, Pallas kernels for 0% -> 0%
where the time goes in v1:
time: 150 us
  Pallas kernels  142 us (95%)
  local copies, waits for them, and re-layouts  7.72 us (5%)
    pallas_call x1, Pallas kernels, shards(): pl.pallas_call(functools.partial(kernel, n_gx, n_gy), out_shape=(jax.Shap...  142 us
    unnamed x16, local copies, waits for them, and re-layouts  7.72 us

profile of v1, /device:TPU:1, one launch (start us, length us, event | category | flops | bytes accessed | tf_op | source)
XLA Modules:
  0.0 149.9 jit_solution(14109484175156304464)
XLA Ops:
  0.6 0.0 copy-start
  0.6 1.3 copy-done
  1.9 0.0 copy-start.1
  1.9 1.3 copy-done.1
  3.2 0.0 copy-start.2
  3.2 0.9 copy-done.2
  4.1 0.0 copy-start.3
  4.1 0.9 copy-done.3
  5.0 0.0 copy-start.4
  5.0 0.7 copy-done.4
  5.7 0.0 copy-start.5
  5.7 0.7 copy-done.5
  6.4 0.0 copy-start.6
  6.4 0.7 copy-done.6
  7.0 141.6 %bddc_cg.1 = (f32[384,128]{1,0:T(8,128)S(1)}, f32[384,128]{1,0:T(8,128)S(1)}) custom-call(bf16[384,128]{1,0:T(8,128)(2,1)S(1)} %bitcast.12, bf16[768,768]{1,0:T(8,128)(2,1)S(1)} %bitcast.8, bf16[768,768]{1,0:T(8,128)(2,1)S(1)} %bitcast.9, bf16[12,768]{1,0:T(8,128)(2,1)S(1)} %bitcast.13, s32[12]{0:T(128)S(1)} %bitcast.14, s32[2]{0:T(128)S(1)} %bitcast.15, ...), custom_call_target="tpu_custom_call" | custom-call | tf_op jit(solution)/shard_map/bddc_cg/pallas_call | solution.py:538
  148.6 0.7 copy.11
  149.3 0.7 copy.12
Async XLA Ops:
  0.6 1.3 copy-start
  1.9 1.3 copy-start.1
  3.2 0.9 copy-start.2
  4.1 0.9 copy-start.3
  5.0 0.7 copy-start.4
  5.7 0.7 copy-start.5
  6.4 0.7 copy-start.6

commit v2 on v1

--- a/solution.py
+++ b/solution.py
@@ -1,4 +1,5 @@
 import functools
+import math
 import jax
 import jax.numpy as jnp
 from jax import lax
@@ -44,6 +45,14 @@
     strip,
     tsel,
     c2,
+    c_own,
+    name_cols,
+    name_lane_msg,
+    tau_strip,
+    tau_low,
+    c_nat,
+    c_line,
+    c_full,
     t_val,
     t_send,
     t_recv,
@@ -71,6 +80,8 @@
     strip_recv,
     c2_send,
     c2_recv,
+    perm_send,
+    perm_recv,
     stage_send,
     stage_recv,
     t_ssem,
@@ -95,26 +106,37 @@
     nc = cr * n_gy
     load_cases = loads.shape[1]
 
-    def plane_peer(k):
-        other = lax.rem(slot + k, n_plane)
-        return {"gx": 2 * z + other // n_gy, "gy": lax.rem(other, n_gy)}
+    side = math.isqrt(n_gy)
+
+    def far_first(step, extent):
+        half = (step + 1) // 2
+        return extent // 2 + jnp.where(lax.rem(step, 2) == 1, -half, half)
+
+    def plane_peer(step, other_core):
+        y = lax.rem(b // side + far_first(step // side, side), side)
+        x = lax.rem(lax.rem(b, side) + far_first(lax.rem(step, side), side), side)
+        return {"gx": 2 * z + lax.rem(c + other_core, 2), "gy": y * side + x}
+
+    def line_peer(step):
+        return lax.rem(z + far_first(step, n_z), n_z)
 
     def signal(device):
         pl.semaphore_signal(barrier, inc=1, device_id=device, device_id_type=MESH)
 
     barrier = pltpu.get_barrier_semaphore()
 
-    @pl.loop(1, n_plane)
-    def _(k):
-        signal(plane_peer(k))
-
-    @pl.loop(1, n_gx)
-    def _(k):
-        other = lax.rem(a + k, n_gx)
-
-        @pl.when(other // 2 != z)
-        def _():
-            signal({"gx": other, "gy": b})
+    @pl.loop(0, n_z - 1)
+    def _(step):
+        other = line_peer(step)
+        signal({"gx": 2 * other, "gy": b})
+        signal({"gx": 2 * other + 1, "gy": b})
+
+    @pl.loop(0, n_gy - 1)
+    def _(step):
+        signal(plane_peer(step, 0))
+        signal(plane_peer(step, 1))
+
+    signal(plane_peer(n_gy - 1, 1))
 
     load_linv = pltpu.make_async_copy(linv_hbm, linv, load_sem.at[0])
     load_schur = pltpu.make_async_copy(schur_hbm, schur, load_sem.at[1])
@@ -132,14 +154,17 @@
         )
 
     def plane_send(src, dst, send, recv):
-        @pl.loop(1, n_plane)
-        def _(k):
-            remote(src, dst.at[slot], send, recv, plane_peer(k)).start()
+        @pl.loop(0, n_gy - 1)
+        def _(step):
+            remote(src, dst.at[slot], send, recv, plane_peer(step, 0)).start()
+            remote(src, dst.at[slot], send, recv, plane_peer(step, 1)).start()
+
+        remote(src, dst.at[slot], send, recv, plane_peer(n_gy - 1, 1)).start()
 
     def z_send(src, dst, send, recv):
-        @pl.loop(1, n_z)
-        def _(k):
-            other = lax.rem(z + k, n_z)
+        @pl.loop(0, n_z - 1)
+        def _(step):
+            other = line_peer(step)
             remote(
                 src.at[other], dst.at[z], send, recv, {"gx": 2 * other + c, "gy": b}
             ).start()
@@ -296,13 +321,21 @@
         yr[k, z] = ys[k, z]
         z_send(ys.at[k], yr.at[k], stage_send.at[k, 3], stage_recv.at[k, 3])
 
-    def sums_of(k):
-        both = xb[k, cc // 8]
-        return [both[j : j + 1, :] for j in range(4)]
+    def coarse_direct(k):
+        wait_bytes(g_buf.at[k], n_plane - 1, stage_recv.at[k, 0])
+        gathered = g_buf[k].reshape(n_plane * TILE, load_cases)
+        part = jnp.dot(c_full[...], gathered, preferred_element_type=F32)
+        at = lax.rem(lax.broadcasted_iota(jnp.int32, part.shape, 0), TILE)
+        rest = part - part.astype(BF16).astype(F32)
+        part = jnp.where((at == n_primal + 1) | (at == n_primal + 3), rest, part)
+        ys[k] = part.astype(BF16).reshape(n_z, TILE, load_cases)
+        yr[k, z] = ys[k, z]
+        z_send(ys.at[k], yr.at[k], stage_send.at[k, 3], stage_recv.at[k, 3])
 
     def coarse_finish(k):
         wait_bytes(yr.at[k], n_z - 1, stage_recv.at[k, 3])
-        picked = jnp.sum(yr[k].astype(F32), axis=0).astype(BF16)
+        total = jnp.sum(yr[k].astype(F32), axis=0)
+        picked = total.astype(BF16)
         for at in range(4):
             pk[k, at, 0:TILE] = picked
         copies = []
@@ -318,7 +351,9 @@
             )
         for copy in copies:
             copy.start()
-        return copies
+        first = total[n_primal : n_primal + 1] + total[n_primal + 1 : n_primal + 2]
+        second = total[n_primal + 2 : n_primal + 3] + total[n_primal + 3 : n_primal + 4]
+        return copies, first, second
 
     def preconditioned(k, faces):
         parts = []
@@ -364,6 +399,38 @@
     wait_bytes(name_gx, n_gx - 1, name_recv.at[1])
     gx_names = name_gx[...].reshape(n_gx * TILE, name_msg.shape[1]).astype(F32)
     gx_names = gx_names[:, 0:1] * 64.0 + gx_names[:, half : half + 1]
+
+    width = c_nat.shape[2]
+    face_cols = 3 * n_gy
+    lanes = lax.broadcasted_iota(jnp.int32, (TILE, width), 1)
+    prim = lax.broadcasted_iota(jnp.int32, (TILE, width), 0)
+    within = 3 * b + lax.rem(prim, 3)
+    low_face = jnp.where(prim < 3, 0, jnp.where(prim < 6, 1, 3))
+    high_face = jnp.where(prim < 6, 2, 4)
+    owned_prim = ((prim >= 3) & (prim < 6)) | ((prim >= 9) & (prim < 12))
+    low_hit = (lanes == low_face * face_cols + within) & (owned_prim | (prim < 3))
+    high_hit = (lanes == high_face * face_cols + within) & owned_prim
+    spread_names = jnp.broadcast_to(gx_names, (n_gx * TILE, width)).reshape(
+        n_gx, TILE, width
+    )
+    lane_names = jnp.sum(
+        jnp.where(low_hit[None], spread_names[:n_z], 0.0)
+        + jnp.where(high_hit[None], spread_names[n_z:], 0.0),
+        axis=1,
+    )
+    name_lane_msg[...] = lane_names
+    name_cols[b] = lane_names
+
+    @pl.loop(1, n_gy)
+    def _(k):
+        remote(
+            name_lane_msg,
+            name_cols.at[b],
+            perm_send.at[0],
+            perm_recv.at[0],
+            {"gx": a, "gy": lax.rem(b + k, n_gy)},
+        ).start()
+
     wait_bytes(strip.reshape(n_gy, cr, strip_w), n_gy - 1, strip_recv)
     chunk = 256 if nc % 256 == 0 else nc // 3
     column = lax.broadcasted_iota(jnp.int32, (1, chunk), 1).astype(F32)
@@ -382,6 +449,24 @@
         tsel.at[1 - c], c2.at[c], c2_send, c2_recv, {"gx": 2 * z + 1 - c, "gy": b}
     )
     c2_copy.start()
+    c_own[a] = tsel[c, pl.ds(pl.multiple_of(z * TILE, TILE), TILE)]
+
+    def send_rows(core, other):
+        remote(
+            tsel.at[core, pl.ds(pl.multiple_of(other * TILE, TILE), TILE)],
+            c_own.at[a],
+            perm_send.at[1],
+            perm_recv.at[1],
+            {"gx": 2 * other + core, "gy": b},
+        ).start()
+
+    @pl.loop(0, n_z - 1)
+    def _(step):
+        other = line_peer(step)
+        send_rows(0, other)
+        send_rows(1, other)
+
+    send_rows(1 - c, z)
 
     coarse_gather(0)
     finish(bt_copies)
@@ -395,8 +480,32 @@
     )
     c2_copy.wait_recv()
     coarse_solve(0)
+
+    wait_bytes(name_cols, n_gy - 1, perm_recv.at[0])
+    col_names = jnp.sum(name_cols[...], axis=0)
+    used = lax.broadcasted_iota(jnp.int32, col_names.shape, 1) < 5 * face_cols
+    col_strip = ((col_names + 0.5) * (1.0 / cc)).astype(jnp.int32)
+    col_low = col_names.astype(jnp.int32) - cc * col_strip
+    tau_strip[...] = col_strip
+    tau_low[...] = jnp.where(used, col_low, -1)
+    wait_bytes(c_own, n_gx - 1, perm_recv.at[1])
+    inner = lax.broadcasted_iota(jnp.int32, (strip_w, 1), 0)
+    strips = lax.broadcasted_iota(jnp.int32, (n_gx, 1, 1), 0)
+
+    @pl.loop(0, n_z)
+    def _(step):
+        picks = jnp.where(inner == tau_low[pl.ds(step, 1), :], 1.0, 0.0).astype(BF16)
+        mine = c_own[...].reshape(n_gx * TILE, strip_w)
+        wide_rows = jnp.dot(mine, picks, preferred_element_type=F32)
+        wide_rows = wide_rows.reshape(n_gx, TILE, width)
+        hit = strips == tau_strip[pl.ds(step, 1), :][None]
+        c_nat[step] = jnp.sum(jnp.where(hit, wide_rows, 0.0), axis=0).astype(BF16)
+
+    c_line[z] = c_nat[z]
+    z_send(c_nat, c_line, perm_send.at[2], perm_recv.at[2])
+
     finish(t_copies[0])
-    pk_copies = [coarse_finish(0)]
+    pk_copies = [coarse_finish(0)[0]]
     finish(pk_copies[0])
     for at, part in enumerate(preconditioned(0, range(4))):
         v0[face_rows(at), :] = part
@@ -410,15 +519,33 @@
     old, curve = owned(start, first), owned(first, image)
 
     t_copies.append(coarse_start(1, image.astype(BF16), [*split(old), *split(curve)]))
-    coarse_scatter(1)
-    coarse_gather(1)
-    coarse_solve(1)
+
+    wait_bytes(c_line, n_z - 1, perm_recv.at[2])
+    at = lax.broadcasted_iota(jnp.int32, (1, n_plane * TILE), 1)
+    at_slot, at_prim = at // TILE, lax.rem(at, TILE)
+    at_core, at_b = at_slot // n_gy, lax.rem(at_slot, n_gy)
+    at_face = jnp.where(
+        at_prim < 3, at_core, jnp.where(at_prim < 6, 1 + at_core, 3 + at_core)
+    )
+    at_b = jnp.where((at_prim >= 6) & (at_prim < 9), lax.rem(at_b + n_gy - 1, n_gy), at_b)
+    at_col = jnp.where(
+        at_prim < 12, at_face * face_cols + 3 * at_b + lax.rem(at_prim, 3), -1
+    )
+    place = jnp.where(
+        lax.broadcasted_iota(jnp.int32, (width, 1), 0) == at_col, 1.0, 0.0
+    ).astype(BF16)
+    block = jnp.dot(
+        c_line[...].reshape(n_z * TILE, width), place, preferred_element_type=F32
+    )
+    row_prim = lax.rem(lax.broadcasted_iota(jnp.int32, (n_z * TILE, 1), 0), TILE)
+    adds = (row_prim >= 12) & (at_prim >= 12) & (row_prim // 2 == at_prim // 2)
+    c_full[...] = jnp.where(adds, 1.0, block).astype(BF16)
+
+    coarse_direct(1)
     finish(t_copies[1])
-    sums = sums_of(1)
-    old = sums[0] + sums[1]
-    curve = sums[2] + sums[3]
+    copies, old, curve = coarse_finish(1)
     step = old / curve
-    pk_copies.append(coarse_finish(1))
+    pk_copies.append(copies)
     finish(pk_copies[1])
     for at, part in enumerate(preconditioned(1, range(4))):
         here = face_rows(at)
@@ -429,20 +556,15 @@
     image, copies = operate(1, second)
     s_copies.append(copies)
     residual = rows[...].astype(F32) - step * w0[...]
-    new = owned(residual, second)
-    cross = owned(second, w0[...])
-    high, low = split(owned(second, image))
-
-    t_copies.append(coarse_start(2, image.astype(BF16), [new, high, low, cross]))
-    coarse_scatter(2)
-    coarse_gather(2)
-    coarse_solve(2)
+    new, second_curve = owned(residual, second), owned(second, image)
+
+    t_copies.append(coarse_start(2, image.astype(BF16), [*split(new), *split(second_curve)]))
+    coarse_direct(2)
     finish(t_copies[2])
-    sums = sums_of(2)
-    new = sums[0]
+    copies, new, second_curve = coarse_finish(2)
     ratio = new / old
-    step_two = new / (sums[1] + sums[2] + ratio * (2.0 * sums[3] + ratio * curve))
-    pk_copies.append(coarse_finish(2))
+    step_two = new / (second_curve - ratio * ratio * curve)
+    pk_copies.append(copies)
     finish(pk_copies[2])
     for half_at, (at, part) in enumerate(zip((1, 3), preconditioned(2, (1, 3)))):
         here = face_rows(at)
@@ -457,12 +579,15 @@
     wait_bytes(name_plane, n_plane - 1, name_send.at[0])
     wait_bytes(name_gx, n_gx - 1, name_send.at[1])
     wait_bytes(strip.reshape(n_gy, cr, strip_w), n_gy - 1, strip_send)
+    wait_bytes(name_cols, n_gy - 1, perm_send.at[0])
+    wait_bytes(c_own, n_gx - 1, perm_send.at[1])
+    wait_bytes(c_line, n_z - 1, perm_send.at[2])
+    wait_bytes(xr.at[0], n_z - 1, stage_send.at[0, 1])
+    wait_bytes(xb.at[0], n_plane - 1, stage_send.at[0, 2])
     for k in range(SOLVES):
         for copy in t_copies[k] + pk_copies[k]:
             copy.wait_send()
         wait_bytes(g_buf.at[k], n_plane - 1, stage_send.at[k, 0])
-        wait_bytes(xr.at[k], n_z - 1, stage_send.at[k, 1])
-        wait_bytes(xb.at[k], n_plane - 1, stage_send.at[k, 2])
         wait_bytes(yr.at[k], n_z - 1, stage_send.at[k, 3])
     for k in range(OPS):
         for copy in s_copies[k]:
@@ -499,6 +624,14 @@
         pltpu.VMEM((nc, strip_w), BF16),
         pltpu.VMEM((2, n_z * TILE, strip_w), BF16),
         pltpu.VMEM((2, n_z * TILE, strip_w), BF16),
+        pltpu.VMEM((n_gx, TILE, strip_w), BF16),
+        pltpu.VMEM((n_gy, n_z, 16 * n_gy), F32),
+        pltpu.VMEM((n_z, 16 * n_gy), F32),
+        pltpu.VMEM((n_z, 16 * n_gy), jnp.int32),
+        pltpu.VMEM((n_z, 16 * n_gy), jnp.int32),
+        pltpu.VMEM((n_z, TILE, 16 * n_gy), BF16),
+        pltpu.VMEM((n_z, TILE, 16 * n_gy), BF16),
+        pltpu.VMEM((n_z * TILE, n_plane * TILE), BF16),
         pltpu.VMEM((local, cases), F32),
         pltpu.VMEM((SOLVES, local, cases), BF16),
         pltpu.VMEM((SOLVES, local, cases), BF16),
@@ -526,6 +659,8 @@
         dma,
         dma,
         dma,
+        dma((3,)),
+        dma((3,)),
         dma((SOLVES, 4)),
         dma((SOLVES, 4)),
         dma((SOLVES, 4)),
@@ -545,7 +680,7 @@
         out_specs=(vmem, vmem),
         scratch_shapes=scratch,
         compiler_params=pltpu.CompilerParams(
-            collective_id=0, has_side_effects=True, vmem_limit_bytes=40 * 1024 * 1024
+            collective_id=0, has_side_effects=True, vmem_limit_bytes=60 * 1024 * 1024
         ),
         name="bddc_cg",
     )(

time: 150 us -> 111 us (0.74)
  Pallas kernels: 142 us -> 107 us
  local copies, waits for them, and re-layouts: 7.72 us -> 3.23 us
    pallas_call x1, Pallas kernels: 142 us -> 107 us  [shards(): pl.pallas_call(functools.partial(kernel, n_gx, n_gy), out_shape=(jax.Shap...]
    unnamed x16 -> x2, local copies, waits for them, and re-layouts: 7.72 us -> 3.23 us
where the time goes in v2:
time: 111 us
  Pallas kernels  107 us (96%)
  local copies, waits for them, and re-layouts  3.23 us (3%)
    pallas_call x1, Pallas kernels, shards(): pl.pallas_call(functools.partial(kernel, n_gx, n_gy), out_shape=(jax.Shap...  107 us
    unnamed x2, local copies, waits for them, and re-layouts  3.23 us

profile of v2, /device:TPU:1, one launch (start us, length us, event | category | flops | bytes accessed | tf_op | source)
XLA Modules:
  0.0 110.8 jit_solution(527655917710758056)
XLA Ops:
  0.6 106.9 %bddc_cg.1 = (f32[384,128]{1,0:T(8,128)}, f32[384,128]{1,0:T(8,128)}) custom-call(bf16[384,128]{1,0:T(8,128)(2,1)} %bitcast.12, bf16[768,768]{1,0:T(8,128)(2,1)} %bitcast.8, bf16[768,768]{1,0:T(8,128)(2,1)} %bitcast.9, bf16[12,768]{1,0:T(8,128)(2,1)} %bitcast.13, s32[12]{0:T(128)} %bitcast.14, s32[2]{0:T(128)} %bitcast.15, f32[192,96]{1,0:T(8,128)} %cinv.1), custom_call_target="tpu_custom_call" | custom-call | tf_op jit(solution)/shard_map/bddc_cg/pallas_call | solution.py:673
  107.5 1.6 %copy.11 = f32[1,1,384,128]{3,2,1,0:T(8,128)} copy(f32[1,1,384,128]{3,2,1,0:T(8,128)} %bitcast.11) | data formatting | bytes 393216
  109.2 1.6 %copy.12 = f32[1,1,384,128]{3,2,1,0:T(8,128)} copy(f32[1,1,384,128]{3,2,1,0:T(8,128)} %bitcast.10) | data formatting | bytes 393216

commit v3 on v2

--- a/solution.py
+++ b/solution.py
@@ -16,6 +16,23 @@
 BT_LANES = 128
 SOLVES = 3
 OPS = 2
+SLOT_LANES = 256
+OFFSETS = (
+    (-1, 0),
+    (1, 0),
+    (0, -1),
+    (0, 1),
+    (-2, 0),
+    (2, 0),
+    (0, -2),
+    (0, 2),
+    (-1, -1),
+    (-1, 1),
+    (1, -1),
+    (1, 1),
+)
+DIAGONALS = OFFSETS[8:]
+SEEN = ((1, 5, 0, 9, 10), (2, 0, 6, 11, 12), (3, 9, 11, 7, 0), (4, 10, 12, 0, 8))
 
 
 def kernel(
@@ -54,10 +71,15 @@
     c_line,
     c_full,
     t_val,
-    t_send,
     t_recv,
-    s_send,
+    t_hat,
+    s_val,
     s_recv,
+    s_hat,
+    sg_send,
+    sg_recv,
+    g_mat,
+    h_mat,
     g_msg,
     g_buf,
     xs,
@@ -88,6 +110,8 @@
     t_rsem,
     s_ssem,
     s_rsem,
+    sg_ssem,
+    sg_rsem,
     p_ssem,
     p_rsem,
 ):
@@ -124,6 +148,7 @@
         pl.semaphore_signal(barrier, inc=1, device_id=device, device_id_type=MESH)
 
     barrier = pltpu.get_barrier_semaphore()
+    pk[...] = jnp.zeros_like(pk)
 
     @pl.loop(0, n_z - 1)
     def _(step):
@@ -137,6 +162,15 @@
         signal(plane_peer(step, 1))
 
     signal(plane_peer(n_gy - 1, 1))
+
+    def grid_peer(offset):
+        return {
+            "gx": lax.rem(a + offset[0] + n_gx, n_gx),
+            "gy": lax.rem(b + offset[1] + n_gy, n_gy),
+        }
+
+    for offset in DIAGONALS:
+        signal(grid_peer(offset))
 
     load_linv = pltpu.make_async_copy(linv_hbm, linv, load_sem.at[0])
     load_schur = pltpu.make_async_copy(schur_hbm, schur, load_sem.at[1])
@@ -247,7 +281,7 @@
     )
     strip[pl.ds(pl.multiple_of(b * cr, 8), cr), :] = wide
 
-    pl.semaphore_wait(barrier, n_plane - 1 + n_gx - 2)
+    pl.semaphore_wait(barrier, n_plane - 1 + n_gx - 2 + len(DIAGONALS))
 
     start_copies = []
     for mine, (device, theirs) in ((1, (east, 0)), (3, (north, 2))):
@@ -290,9 +324,23 @@
         g_msg[k] = message
         g_buf[k, slot] = message
         plane_send(g_msg.at[k], g_buf.at[k], stage_send.at[k, 0], stage_recv.at[k, 0])
-        t_val[...] = jnp.dot(linv[...], local_rows, preferred_element_type=F32)
-        t_send[k] = t_val[...].astype(BF16)
-        return exchange(t_send.at[k], t_recv.at[k], t_ssem.at[k], t_rsem.at[k])
+        t_val[k] = jnp.dot(linv[...], local_rows, preferred_element_type=F32)
+        return exchange(t_val.at[k], t_recv.at[k], t_ssem.at[k], t_rsem.at[k])
+
+    def operate(k):
+        finish(t_copies[k])
+        joined = (t_val[k] + t_recv[k]) * masks[...]
+        t_hat[k] = joined
+        high = joined.astype(BF16)
+        rest = (joined - high.astype(F32)).astype(BF16)
+        s_val[k] = jnp.dot(schur[...], high, preferred_element_type=F32) + jnp.dot(
+            schur[...], rest, preferred_element_type=F32
+        )
+        return exchange(s_val.at[k], s_recv.at[k], s_ssem.at[k], s_rsem.at[k])
+
+    def operated(k):
+        finish(s_copies[k])
+        s_hat[k] = (s_val[k] + s_recv[k]) * masks[...]
 
     def coarse_scatter(k):
         wait_bytes(g_buf.at[k], n_plane - 1, stage_recv.at[k, 0])
@@ -335,41 +383,25 @@
     def coarse_finish(k):
         wait_bytes(yr.at[k], n_z - 1, stage_recv.at[k, 3])
         total = jnp.sum(yr[k].astype(F32), axis=0)
-        picked = total.astype(BF16)
-        for at in range(4):
-            pk[k, at, 0:TILE] = picked
-        copies = []
-        for mine, (device, theirs) in enumerate(neighbours):
-            copies.append(
+        pk[k, 0:TILE] = total.astype(BF16)
+        offsets = OFFSETS if k + 1 < SOLVES else OFFSETS[:4:2]
+        for at, offset in enumerate(OFFSETS):
+            if offset in offsets:
+                back = OFFSETS.index((-offset[0], -offset[1]))
                 remote(
-                    pk.at[k, mine, pl.ds(0, TILE)],
-                    pk.at[k, theirs, pl.ds(TILE, TILE)],
-                    p_ssem.at[k, mine],
-                    p_rsem.at[k, theirs],
-                    device,
-                )
-            )
-        for copy in copies:
-            copy.start()
+                    pk.at[k, pl.ds(0, TILE)],
+                    pk.at[k, pl.ds((1 + back) * TILE, TILE)],
+                    p_ssem.at[k],
+                    p_rsem.at[k],
+                    grid_peer(offset),
+                ).start()
         first = total[n_primal : n_primal + 1] + total[n_primal + 1 : n_primal + 2]
         second = total[n_primal + 2 : n_primal + 3] + total[n_primal + 3 : n_primal + 4]
-        return copies, first, second
-
-    def preconditioned(k, faces):
-        parts = []
-        for at in faces:
-            here = face_rows(at)
-            spread = jnp.dot(bb[here, 0 : 2 * TILE], pk[k, at], preferred_element_type=F32)
-            total = t_val[here, :] + t_recv[k, here, :].astype(F32) + spread
-            parts.append(total * masks[here, :])
-        return parts
-
-    def operate(k, vector):
-        mapped = jnp.dot(schur[...], vector.astype(BF16), preferred_element_type=F32)
-        s_send[k] = mapped.astype(BF16)
-        copies = exchange(s_send.at[k], s_recv.at[k], s_ssem.at[k], s_rsem.at[k])
-        finish(copies)
-        return (mapped + s_recv[k].astype(F32)) * masks[...], copies
+        return len(offsets), first, second
+
+    def wait_tiles(k, count, sem):
+        part = pk.at[k, pl.ds(TILE, count * TILE)]
+        pltpu.make_async_copy(part, part, sem.at[k]).wait()
 
     def owned(first, second):
         total = first * second
@@ -383,7 +415,9 @@
 
     finish(start_copies)
     load_linv.wait()
-    t_copies = [coarse_start(0, rows[...], [])]
+    t_copies = []
+    s_copies = []
+    t_copies.append(coarse_start(0, rows[...], []))
 
     wait_bytes(name_plane, n_plane - 1, name_recv.at[0])
     plane_names = name_plane[...].reshape(n_plane * TILE, name_msg.shape[1]).astype(F32)
@@ -468,7 +502,6 @@
 
     send_rows(1 - c, z)
 
-    coarse_gather(0)
     finish(bt_copies)
     bb[...] = bb[...] + bt_recv[...]
     masks[0:face, :] = jnp.broadcast_to(
@@ -478,6 +511,23 @@
         bt_recv[2 * face : 3 * face, MASK_LANE : MASK_LANE + 1].astype(F32),
         (face, load_cases),
     )
+    load_schur.wait()
+    s_copies.append(operate(0))
+    coarse_gather(0)
+
+    from_row = lax.broadcasted_iota(jnp.int32, (BT_LANES, SLOT_LANES), 0)
+    to_lane = lax.broadcasted_iota(jnp.int32, (BT_LANES, SLOT_LANES), 1)
+    for at in range(4):
+        to_slot = jnp.where(from_row < TILE, 0, at + 1)
+        hit = (to_lane == TILE * to_slot + lax.rem(from_row, TILE)) & (from_row < 2 * TILE)
+        move = jnp.where(hit, 1.0, 0.0).astype(BF16)
+        here = face_rows(at)
+        moved = jnp.dot(bb[here, :], move, preferred_element_type=F32)
+        g_mat[here, :] = jnp.where(masks[here, 0:1] > 0.5, moved, 0.0).astype(BF16)
+    image = jnp.dot(schur[...], g_mat[:, 0:BT_LANES], preferred_element_type=F32)
+    sg_send[...] = image.astype(BF16)
+    sg_copies = exchange(sg_send, sg_recv, sg_ssem, sg_rsem)
+
     c2_copy.wait_recv()
     coarse_solve(0)
 
@@ -504,16 +554,25 @@
     c_line[z] = c_nat[z]
     z_send(c_nat, c_line, perm_send.at[2], perm_recv.at[2])
 
-    finish(t_copies[0])
-    pk_copies = [coarse_finish(0)[0]]
-    finish(pk_copies[0])
-    for at, part in enumerate(preconditioned(0, range(4))):
-        v0[face_rows(at), :] = part
-
-    load_schur.wait()
-    first = v0[...]
-    image, copies = operate(0, first)
-    s_copies = [copies]
+    finish(sg_copies)
+    for at in range(4):
+        to_slot = jnp.full(from_row.shape, -1, jnp.int32)
+        for mine, theirs in enumerate(SEEN[at]):
+            to_slot = jnp.where(from_row // TILE == mine, theirs, to_slot)
+        hit = to_lane == TILE * to_slot + lax.rem(from_row, TILE)
+        move = jnp.where(hit & (to_slot >= 0), 1.0, 0.0).astype(BF16)
+        here = face_rows(at)
+        moved = jnp.dot(sg_recv[here, :], move, preferred_element_type=F32)
+        stay = jnp.where(to_lane == from_row, 1.0, 0.0).astype(BF16)
+        kept = jnp.dot(sg_send[here, :], stay, preferred_element_type=F32)
+        h_mat[here, :] = jnp.where(masks[here, 0:1] > 0.5, moved + kept, 0.0).astype(BF16)
+    operated(0)
+
+    counts = [coarse_finish(0)[0]]
+    wait_tiles(0, counts[0], p_rsem)
+    first = t_hat[0] + jnp.dot(g_mat[...], pk[0], preferred_element_type=F32)
+    image = s_hat[0] + jnp.dot(h_mat[...], pk[0], preferred_element_type=F32)
+    v0[...] = first
     w0[...] = image
     start = rows[...].astype(F32)
     old, curve = owned(start, first), owned(first, image)
@@ -542,39 +601,41 @@
     c_full[...] = jnp.where(adds, 1.0, block).astype(BF16)
 
     coarse_direct(1)
-    finish(t_copies[1])
-    copies, old, curve = coarse_finish(1)
+    s_copies.append(operate(1))
+    count, old, curve = coarse_finish(1)
     step = old / curve
-    pk_copies.append(copies)
-    finish(pk_copies[1])
-    for at, part in enumerate(preconditioned(1, range(4))):
-        here = face_rows(at)
-        v1[here, :] = part
-        z1[here, :] = v0[here, :] - step * part
-
-    second = z1[...]
-    image, copies = operate(1, second)
-    s_copies.append(copies)
+    counts.append(count)
+    operated(1)
+    wait_tiles(1, count, p_rsem)
+    part = t_hat[1] + jnp.dot(g_mat[...], pk[1], preferred_element_type=F32)
+    v1[...] = part
+    second = v0[...] - step * part
+    z1[...] = second
+    image = s_hat[1] + jnp.dot(h_mat[...], pk[1], preferred_element_type=F32)
+    image = w0[...] - step * image
     residual = rows[...].astype(F32) - step * w0[...]
     new, second_curve = owned(residual, second), owned(second, image)
 
     t_copies.append(coarse_start(2, image.astype(BF16), [*split(new), *split(second_curve)]))
     coarse_direct(2)
     finish(t_copies[2])
-    copies, new, second_curve = coarse_finish(2)
+    count, new, second_curve = coarse_finish(2)
     ratio = new / old
     step_two = new / (second_curve - ratio * ratio * curve)
-    pk_copies.append(copies)
-    finish(pk_copies[2])
-    for half_at, (at, part) in enumerate(zip((1, 3), preconditioned(2, (1, 3)))):
+    counts.append(count)
+    wait_tiles(2, count, p_rsem)
+    for half_at, at in enumerate((1, 3)):
         here = face_rows(at)
         there = pl.ds(half_at * face, face)
+        part = (t_val[2, here, :] + t_recv[2, here, :]) * masks[here, :] + jnp.dot(
+            g_mat[here, :], pk[2], preferred_element_type=F32
+        )
         second = z1[here, :]
         direction = second + ratio * v0[here, :]
         sol_out[there, :] = step * v0[here, :] + step_two * direction
         pre_out[there, :] = second - step_two * (part + ratio * v1[here, :])
 
-    for copy in start_copies + bt_copies + [c2_copy]:
+    for copy in start_copies + bt_copies + [c2_copy] + sg_copies:
         copy.wait_send()
     wait_bytes(name_plane, n_plane - 1, name_send.at[0])
     wait_bytes(name_gx, n_gx - 1, name_send.at[1])
@@ -585,8 +646,9 @@
     wait_bytes(xr.at[0], n_z - 1, stage_send.at[0, 1])
     wait_bytes(xb.at[0], n_plane - 1, stage_send.at[0, 2])
     for k in range(SOLVES):
-        for copy in t_copies[k] + pk_copies[k]:
+        for copy in t_copies[k]:
             copy.wait_send()
+        wait_tiles(k, counts[k], p_ssem)
         wait_bytes(g_buf.at[k], n_plane - 1, stage_send.at[k, 0])
         wait_bytes(yr.at[k], n_z - 1, stage_send.at[k, 3])
     for k in range(OPS):
@@ -632,11 +694,16 @@
         pltpu.VMEM((n_z, TILE, 16 * n_gy), BF16),
         pltpu.VMEM((n_z, TILE, 16 * n_gy), BF16),
         pltpu.VMEM((n_z * TILE, n_plane * TILE), BF16),
-        pltpu.VMEM((local, cases), F32),
-        pltpu.VMEM((SOLVES, local, cases), BF16),
-        pltpu.VMEM((SOLVES, local, cases), BF16),
-        pltpu.VMEM((OPS, local, cases), BF16),
-        pltpu.VMEM((OPS, local, cases), BF16),
+        pltpu.VMEM((SOLVES, local, cases), F32),
+        pltpu.VMEM((SOLVES, local, cases), F32),
+        pltpu.VMEM((OPS, local, cases), F32),
+        pltpu.VMEM((OPS, local, cases), F32),
+        pltpu.VMEM((OPS, local, cases), F32),
+        pltpu.VMEM((OPS, local, cases), F32),
+        pltpu.VMEM((local, BT_LANES), BF16),
+        pltpu.VMEM((local, BT_LANES), BF16),
+        pltpu.VMEM((local, SLOT_LANES), BF16),
+        pltpu.VMEM((local, SLOT_LANES), BF16),
         pltpu.VMEM((SOLVES, TILE, cases), BF16),
         pltpu.VMEM((SOLVES, n_plane, TILE, cases), BF16),
         pltpu.VMEM((SOLVES, n_z, 8, cases), F32),
@@ -645,7 +712,7 @@
         pltpu.VMEM((SOLVES, n_plane, 8, cases), F32),
         pltpu.VMEM((SOLVES, n_z, TILE, cases), BF16),
         pltpu.VMEM((SOLVES, n_z, TILE, cases), BF16),
-        pltpu.VMEM((SOLVES, 4, 2 * TILE, cases), BF16),
+        pltpu.VMEM((SOLVES, SLOT_LANES, cases), BF16),
         pltpu.VMEM((local, cases), F32),
         pltpu.VMEM((local, cases), F32),
         pltpu.VMEM((local, cases), F32),
@@ -667,8 +734,10 @@
         dma((SOLVES, 4)),
         dma((OPS, 4)),
         dma((OPS, 4)),
-        dma((SOLVES, 4)),
-        dma((SOLVES, 4)),
+        dma((4,)),
+        dma((4,)),
+        dma((SOLVES,)),
+        dma((SOLVES,)),
     ]
     solution, precond = pl.pallas_call(
         functools.partial(kernel, n_gx, n_gy),

time: 111 us -> 103 us (0.928)
  Pallas kernels: 107 us -> 98.5 us
    pallas_call x1, Pallas kernels: 107 us -> 98.5 us  [shards(): pl.pallas_call(functools.partial(kernel, n_gx, n_gy), out_shape=(jax.Shap...]
where the time goes in v3:
time: 103 us; the launch traced here: 102 us
  Pallas kernels  98.5 us (96%)
  local copies, waits for them, and re-layouts  3.23 us (3%)
    pallas_call x1, Pallas kernels, shards(): pl.pallas_call(functools.partial(kernel, n_gx, n_gy), out_shape=(jax.Shap...  98.5 us
    unnamed x2, local copies, waits for them, and re-layouts  3.23 us

profile of v3, /device:TPU:1, one launch (start us, length us, event | category | flops | bytes accessed | tf_op | source)
XLA Modules:
  0.0 102.4 jit_solution(3574277607066228097)
XLA Ops:
  0.6 98.5 %bddc_cg.1 = (f32[384,128]{1,0:T(8,128)}, f32[384,128]{1,0:T(8,128)}) custom-call(bf16[384,128]{1,0:T(8,128)(2,1)} %bitcast.12, bf16[768,768]{1,0:T(8,128)(2,1)} %bitcast.8, bf16[768,768]{1,0:T(8,128)(2,1)} %bitcast.9, bf16[12,768]{1,0:T(8,128)(2,1)} %bitcast.13, s32[12]{0:T(128)} %bitcast.14, s32[2]{0:T(128)} %bitcast.15, f32[192,96]{1,0:T(8,128)} %cinv.1), custom_call_target="tpu_custom_call" | custom-call | tf_op jit(solution)/shard_map/bddc_cg/pallas_call | solution.py:742
  99.1 1.6 %copy.11 = f32[1,1,384,128]{3,2,1,0:T(8,128)} copy(f32[1,1,384,128]{3,2,1,0:T(8,128)} %bitcast.11) | data formatting | bytes 393216
  100.8 1.6 %copy.12 = f32[1,1,384,128]{3,2,1,0:T(8,128)} copy(f32[1,1,384,128]{3,2,1,0:T(8,128)} %bitcast.10) | data formatting | bytes 393216

commit v4 on v3

--- a/solution.py
+++ b/solution.py
@@ -59,7 +59,8 @@
     name_plane,
     name_gx,
     sel_t,
-    strip,
+    strip_x,
+    strip_y,
     tsel,
     c2,
     c_own,
@@ -127,7 +128,6 @@
     nodes_per = face // 3
     cr, cc = cinv.shape
     strip_w = 8 * n_gy
-    nc = cr * n_gy
     load_cases = loads.shape[1]
 
     side = math.isqrt(n_gy)
@@ -275,11 +275,13 @@
     name_plane[slot] = name_msg[...]
     name_gx[c * n_z + z] = name_msg[...]
 
-    my_strip = strip.at[pl.ds(pl.multiple_of(b * cr, 8), cr)]
+    half_cr = cr // 2
+    row_y, row_x = b // side, lax.rem(b, side)
     wide = jnp.concatenate(
         [cinv[...].astype(BF16), jnp.zeros((cr, strip_w - cc), BF16)], axis=1
     )
-    strip[pl.ds(pl.multiple_of(b * cr, 8), cr), :] = wide
+    strip_x[b] = wide[:half_cr]
+    strip_y[row_x * side + row_y] = wide[half_cr:]
 
     pl.semaphore_wait(barrier, n_plane - 1 + n_gx - 2 + len(DIAGONALS))
 
@@ -308,12 +310,33 @@
             {"gx": other, "gy": b},
         ).start()
 
-    @pl.loop(1, n_gy)
-    def _(k):
-        other = lax.rem(b + k, n_gy)
-        remote(my_strip, my_strip, strip_send, strip_recv, {"gx": a, "gy": other}).start()
-
-    bt_copies = exchange(bt_send, bt_recv, face_send.at[pl.ds(4, 4)], face_recv.at[pl.ds(4, 4)])
+    def along_x(step):
+        x = lax.rem(row_x + far_first(step, side), side)
+        return {"gx": a, "gy": row_y * side + x}
+
+    def along_y(step):
+        y = lax.rem(row_y + far_first(step, side), side)
+        return {"gx": a, "gy": y * side + row_x}
+
+    def strip_pass(which, first_x, count_x, first_y, count_y):
+        here_x = strip_x.at[pl.ds(first_x, count_x)]
+        here_y = strip_y.at[pl.ds(first_y, count_y)]
+        ways = (along_x, along_y) if which == 0 else (along_y, along_x)
+
+        @pl.loop(0, side - 1)
+        def _(step):
+            at = 2 * which
+            remote(here_x, here_x, strip_send.at[at], strip_recv.at[at], ways[0](step)).start()
+            remote(
+                here_y, here_y, strip_send.at[at + 1], strip_recv.at[at + 1], ways[1](step)
+            ).start()
+
+    def strip_wait(which, sem):
+        count = (side - 1) * (side if which else 1)
+        wait_bytes(strip_x, count, sem.at[2 * which])
+        wait_bytes(strip_y, count, sem.at[2 * which + 1])
+
+    strip_pass(0, b, 1, row_x * side + row_y, 1)
 
     def coarse_start(k, local_rows, sums):
         primal = jnp.dot(basis16, local_rows, preferred_element_type=F32)
@@ -324,7 +347,12 @@
         g_msg[k] = message
         g_buf[k, slot] = message
         plane_send(g_msg.at[k], g_buf.at[k], stage_send.at[k, 0], stage_recv.at[k, 0])
+        if k == 0:
+            strip_wait(0, strip_recv)
+            strip_pass(1, row_y * side, side, row_x * side, side)
         t_val[k] = jnp.dot(linv[...], local_rows, preferred_element_type=F32)
+
+    def local_start(k):
         return exchange(t_val.at[k], t_recv.at[k], t_ssem.at[k], t_rsem.at[k])
 
     def operate(k):
@@ -417,7 +445,7 @@
     load_linv.wait()
     t_copies = []
     s_copies = []
-    t_copies.append(coarse_start(0, rows[...], []))
+    coarse_start(0, rows[...], [])
 
     wait_bytes(name_plane, n_plane - 1, name_recv.at[0])
     plane_names = name_plane[...].reshape(n_plane * TILE, name_msg.shape[1]).astype(F32)
@@ -429,6 +457,9 @@
     sel_t[...] = hits.T.astype(BF16)
 
     coarse_scatter(0)
+    bt_copies = exchange(bt_send, bt_recv, face_send.at[pl.ds(4, 4)], face_recv.at[pl.ds(4, 4)])
+
+    t_copies.append(local_start(0))
 
     wait_bytes(name_gx, n_gx - 1, name_recv.at[1])
     gx_names = name_gx[...].reshape(n_gx * TILE, name_msg.shape[1]).astype(F32)
@@ -465,17 +496,26 @@
             {"gx": a, "gy": lax.rem(b + k, n_gy)},
         ).start()
 
-    wait_bytes(strip.reshape(n_gy, cr, strip_w), n_gy - 1, strip_recv)
-    chunk = 256 if nc % 256 == 0 else nc // 3
-    column = lax.broadcasted_iota(jnp.int32, (1, chunk), 1).astype(F32)
+    strip_wait(1, strip_recv)
+    column = lax.broadcasted_iota(jnp.int32, (1, cr), 1)
+    second_half = column >= half_cr
 
     def select(step, total):
-        base = pl.multiple_of(step * chunk, chunk)
-        hit = jnp.where(gx_names - (base * 1.0) == column, 1.0, 0.0).astype(BF16)
-        return total + jnp.dot(hit, strip[pl.ds(base, chunk), :], preferred_element_type=F32)
+        at = 2 * step
+        at_x = jnp.where(second_half, cr * (at + 1) + column - half_cr, cr * at + column)
+        low = lax.rem(at, side) * side + at // side
+        at_y = jnp.where(
+            second_half, cr * (low + side) + column, cr * low + column + half_cr
+        )
+        hit_x = jnp.where(gx_names == at_x.astype(F32), 1.0, 0.0).astype(BF16)
+        hit_y = jnp.where(gx_names == at_y.astype(F32), 1.0, 0.0).astype(BF16)
+        rows_x = strip_x[pl.ds(at, 2)].reshape(cr, strip_w)
+        rows_y = strip_y[pl.ds(at, 2)].reshape(cr, strip_w)
+        total = total + jnp.dot(hit_x, rows_x, preferred_element_type=F32)
+        return total + jnp.dot(hit_y, rows_y, preferred_element_type=F32)
 
     chosen = lax.fori_loop(
-        0, nc // chunk, select, jnp.zeros((n_gx * TILE, strip_w), F32)
+        0, n_gy // 2, select, jnp.zeros((n_gx * TILE, strip_w), F32)
     )
     tsel[...] = chosen.astype(BF16).reshape(2, n_z * TILE, strip_w)
     c2[c] = tsel[c]
@@ -502,6 +542,7 @@
 
     send_rows(1 - c, z)
 
+    coarse_gather(0)
     finish(bt_copies)
     bb[...] = bb[...] + bt_recv[...]
     masks[0:face, :] = jnp.broadcast_to(
@@ -513,7 +554,6 @@
     )
     load_schur.wait()
     s_copies.append(operate(0))
-    coarse_gather(0)
 
     from_row = lax.broadcasted_iota(jnp.int32, (BT_LANES, SLOT_LANES), 0)
     to_lane = lax.broadcasted_iota(jnp.int32, (BT_LANES, SLOT_LANES), 1)
@@ -577,7 +617,8 @@
     start = rows[...].astype(F32)
     old, curve = owned(start, first), owned(first, image)
 
-    t_copies.append(coarse_start(1, image.astype(BF16), [*split(old), *split(curve)]))
+    coarse_start(1, image.astype(BF16), [*split(old), *split(curve)])
+    t_copies.append(local_start(1))
 
     wait_bytes(c_line, n_z - 1, perm_recv.at[2])
     at = lax.broadcasted_iota(jnp.int32, (1, n_plane * TILE), 1)
@@ -616,7 +657,8 @@
     residual = rows[...].astype(F32) - step * w0[...]
     new, second_curve = owned(residual, second), owned(second, image)
 
-    t_copies.append(coarse_start(2, image.astype(BF16), [*split(new), *split(second_curve)]))
+    coarse_start(2, image.astype(BF16), [*split(new), *split(second_curve)])
+    t_copies.append(local_start(2))
     coarse_direct(2)
     finish(t_copies[2])
     count, new, second_curve = coarse_finish(2)
@@ -639,7 +681,8 @@
         copy.wait_send()
     wait_bytes(name_plane, n_plane - 1, name_send.at[0])
     wait_bytes(name_gx, n_gx - 1, name_send.at[1])
-    wait_bytes(strip.reshape(n_gy, cr, strip_w), n_gy - 1, strip_send)
+    strip_wait(0, strip_send)
+    strip_wait(1, strip_send)
     wait_bytes(name_cols, n_gy - 1, perm_send.at[0])
     wait_bytes(c_own, n_gx - 1, perm_send.at[1])
     wait_bytes(c_line, n_z - 1, perm_send.at[2])
@@ -662,7 +705,6 @@
     owned, cases = loads.shape[2:]
     local = schur.shape[-1]
     cr, cc = coarse_inverse.shape
-    nc = cr * n_gy
     n_z = n_gx // 2
     n_plane = 2 * n_gy
     strip_w = 8 * n_gy
@@ -683,7 +725,8 @@
         pltpu.VMEM((n_plane, TILE, 128), BF16),
         pltpu.VMEM((n_gx, TILE, 128), BF16),
         pltpu.VMEM((8 * n_z, n_plane * TILE), BF16),
-        pltpu.VMEM((nc, strip_w), BF16),
+        pltpu.VMEM((n_gy, cr // 2, strip_w), BF16),
+        pltpu.VMEM((n_gy, cr // 2, strip_w), BF16),
         pltpu.VMEM((2, n_z * TILE, strip_w), BF16),
         pltpu.VMEM((2, n_z * TILE, strip_w), BF16),
         pltpu.VMEM((n_gx, TILE, strip_w), BF16),
@@ -722,8 +765,8 @@
         dma((8,)),
         dma((2,)),
         dma((2,)),
-        dma,
-        dma,
+        dma((4,)),
+        dma((4,)),
         dma,
         dma,
         dma((3,)),

time: 103 us -> 95.7 us (0.929)
  Pallas kernels: 98.5 us -> 91.6 us
    pallas_call x1, Pallas kernels: 98.5 us -> 91.6 us  [shards(): pl.pallas_call(functools.partial(kernel, n_gx, n_gy), out_shape=(jax.Shap...]
where the time goes in v4:
time: 95.7 us; the launch traced here: 95.5 us
  Pallas kernels  91.6 us (96%)
  local copies, waits for them, and re-layouts  3.23 us (3%)
    pallas_call x1, Pallas kernels, shards(): pl.pallas_call(functools.partial(kernel, n_gx, n_gy), out_shape=(jax.Shap...  91.6 us
    unnamed x2, local copies, waits for them, and re-layouts  3.23 us

profile of v4, /device:TPU:1, one launch (start us, length us, event | category | flops | bytes accessed | tf_op | source)
XLA Modules:
  0.0 95.5 jit_solution(1392020130755659693)
XLA Ops:
  0.6 91.6 %bddc_cg.1 = (f32[384,128]{1,0:T(8,128)}, f32[384,128]{1,0:T(8,128)}) custom-call(bf16[384,128]{1,0:T(8,128)(2,1)} %bitcast.12, bf16[768,768]{1,0:T(8,128)(2,1)} %bitcast.8, bf16[768,768]{1,0:T(8,128)(2,1)} %bitcast.9, bf16[12,768]{1,0:T(8,128)(2,1)} %bitcast.13, s32[12]{0:T(128)} %bitcast.14, s32[2]{0:T(128)} %bitcast.15, f32[192,96]{1,0:T(8,128)} %cinv.1), custom_call_target="tpu_custom_call" | custom-call | tf_op jit(solution)/shard_map/bddc_cg/pallas_call | solution.py:785
  92.2 1.6 %copy.11 = f32[1,1,384,128]{3,2,1,0:T(8,128)} copy(f32[1,1,384,128]{3,2,1,0:T(8,128)} %bitcast.11) | data formatting | bytes 393216
  93.9 1.6 %copy.12 = f32[1,1,384,128]{3,2,1,0:T(8,128)} copy(f32[1,1,384,128]{3,2,1,0:T(8,128)} %bitcast.10) | data formatting | bytes 393216

commit v5 on v4

--- a/solution.py
+++ b/solution.py
@@ -134,11 +134,13 @@
 
     def far_first(step, extent):
         half = (step + 1) // 2
+        if isinstance(step, int):
+            return extent // 2 + (-half if step % 2 else half)
         return extent // 2 + jnp.where(lax.rem(step, 2) == 1, -half, half)
 
     def plane_peer(step, other_core):
         y = lax.rem(b // side + far_first(step // side, side), side)
-        x = lax.rem(lax.rem(b, side) + far_first(lax.rem(step, side), side), side)
+        x = lax.rem(lax.rem(b, side) + far_first(step % side, side), side)
         return {"gx": 2 * z + lax.rem(c + other_core, 2), "gy": y * side + x}
 
     def line_peer(step):
@@ -188,16 +190,14 @@
         )
 
     def plane_send(src, dst, send, recv):
-        @pl.loop(0, n_gy - 1)
-        def _(step):
+        for step in range(n_gy - 1):
             remote(src, dst.at[slot], send, recv, plane_peer(step, 0)).start()
             remote(src, dst.at[slot], send, recv, plane_peer(step, 1)).start()
 
         remote(src, dst.at[slot], send, recv, plane_peer(n_gy - 1, 1)).start()
 
     def z_send(src, dst, send, recv):
-        @pl.loop(0, n_z - 1)
-        def _(step):
+        for step in range(n_z - 1):
             other = line_peer(step)
             remote(
                 src.at[other], dst.at[z], send, recv, {"gx": 2 * other + c, "gy": b}
@@ -216,9 +216,10 @@
     def face_rows(which):
         return pl.ds(which * face, face)
 
-    def exchange(src, dst, send, recv):
+    def exchange(src, dst, send, recv, faces=(0, 1, 2, 3)):
         copies = []
-        for mine, (device, theirs) in enumerate(neighbours):
+        for mine in faces:
+            device, theirs = neighbours[mine]
             copies.append(
                 remote(
                     src.at[face_rows(mine)],
@@ -353,7 +354,8 @@
         t_val[k] = jnp.dot(linv[...], local_rows, preferred_element_type=F32)
 
     def local_start(k):
-        return exchange(t_val.at[k], t_recv.at[k], t_ssem.at[k], t_rsem.at[k])
+        faces = (0, 1, 2, 3) if k + 1 < SOLVES else (0, 2)
+        return exchange(t_val.at[k], t_recv.at[k], t_ssem.at[k], t_rsem.at[k], faces)
 
     def operate(k):
         finish(t_copies[k])
@@ -413,7 +415,7 @@
         total = jnp.sum(yr[k].astype(F32), axis=0)
         pk[k, 0:TILE] = total.astype(BF16)
         offsets = OFFSETS if k + 1 < SOLVES else OFFSETS[:4:2]
-        for at, offset in enumerate(OFFSETS):
+        for offset in reversed(OFFSETS):
             if offset in offsets:
                 back = OFFSETS.index((-offset[0], -offset[1]))
                 remote(
@@ -658,8 +660,8 @@
     new, second_curve = owned(residual, second), owned(second, image)
 
     coarse_start(2, image.astype(BF16), [*split(new), *split(second_curve)])
+    coarse_direct(2)
     t_copies.append(local_start(2))
-    coarse_direct(2)
     finish(t_copies[2])
     count, new, second_curve = coarse_finish(2)
     ratio = new / old

time: 95.7 us -> 95.2 us (level)
  no operation moved by 1% of the time
where the time goes in v5:
time: 95.2 us; the launch traced here: 95 us
  Pallas kernels  91.2 us (96%)
  local copies, waits for them, and re-layouts  3.23 us (3%)
    pallas_call x1, Pallas kernels, shards(): pl.pallas_call(functools.partial(kernel, n_gx, n_gy), out_shape=(jax.Shap...  91.2 us
    unnamed x2, local copies, waits for them, and re-layouts  3.23 us

profile of v5, /device:TPU:1, one launch (start us, length us, event | category | flops | bytes accessed | tf_op | source)
XLA Modules:
  0.0 95.0 jit_solution(13844810322334644450)
XLA Ops:
  0.6 91.2 %bddc_cg.1 = (f32[384,128]{1,0:T(8,128)}, f32[384,128]{1,0:T(8,128)}) custom-call(bf16[384,128]{1,0:T(8,128)(2,1)} %bitcast.12, bf16[768,768]{1,0:T(8,128)(2,1)} %bitcast.8, bf16[768,768]{1,0:T(8,128)(2,1)} %bitcast.9, bf16[12,768]{1,0:T(8,128)(2,1)} %bitcast.13, s32[12]{0:T(128)} %bitcast.14, s32[2]{0:T(128)} %bitcast.15, f32[192,96]{1,0:T(8,128)} %cinv.1), custom_call_target="tpu_custom_call" | custom-call | tf_op jit(solution)/shard_map/bddc_cg/pallas_call | solution.py:787
  91.8 1.6 %copy.11 = f32[1,1,384,128]{3,2,1,0:T(8,128)} copy(f32[1,1,384,128]{3,2,1,0:T(8,128)} %bitcast.11) | data formatting | bytes 393216
  93.4 1.6 %copy.12 = f32[1,1,384,128]{3,2,1,0:T(8,128)} copy(f32[1,1,384,128]{3,2,1,0:T(8,128)} %bitcast.10) | data formatting | bytes 393216
